TPU v7x, 128 devices: a whole 4x4x4 slice. The times are simulated.
128 devices in a mesh: row: 8 (over x, z_lo), col: 16 (over y, z_hi, core).
Axes of the slice: x: 4, y: 4, z: 4 (z_hi: 2, z_lo: 2; z = z_hi * 2 + z_lo), core: 2. Of those that a mesh axis runs over, the one named last changes fastest.
Arguments:
- left_factors: bfloat16 [32, 2688, 256], P('row', 'col'), may hold values from -0.59765625 to 0.59765625
- right_factors: bfloat16 [32, 2688, 256], P('row', 'col'), may hold values from -0.5 to 0.5
- ranks: int32 [32], replicated, may hold values from 16 to 256, as said below
Outputs:
- offdiag_update: bfloat16 [32, 32, 2688, 256], P('row', 'col')
- diag_update: bfloat16 [32, 2688, 2688], P('row', 'col')
Inputs may be any that keep to these rules, and one draw needn't show every extreme that they name: `ranks`: A tile whose number rnum(p) is 16 or more has rank at most 128, and one such tile has rank exactly 128; some tile of a smaller number has rank 256.
All inputs are finite; a program needn't handle non-finite values.
Results may differ from a plain program's by a relative error of at most 0.0055.
Values may be sent and summed in bfloat16 or wider, within the bound.
No kernel may reach another device: no remote copies, remote signals or barrier semaphores. Data moves between devices by JAX's collectives and lax.ppermute only.
A program may use at most 128 MiB of HBM per device.

v0:
```python
import itertools

import jax
import jax.numpy as jnp
from jax import lax
from jax.experimental import pallas as pl
from jax.experimental.pallas import tpu as pltpu
from jax.sharding import PartitionSpec as P

AXES = ("row", "col")
BF, F32 = jnp.bfloat16, jnp.float32
PTS, CHIP, NB, LIMIT = 168, 336, 2688, 24 * 1024 * 1024


def place(x, zl, y, zh, core):
    return ((x % 4) * 2 + zl) * 16 + (y % 4) * 4 + zh * 2 + core


def mover(rule):
    ranges = (range(4), range(2), range(4), range(2), range(2))
    pairs = [(place(*d), place(*rule(*d))) for d in itertools.product(*ranges)]
    return lambda block: lax.ppermute(block, AXES, pairs)


y_split = mover(lambda x, zl, y, zh, c: (x, zl, y + 1 - 2 * c, zh, c))
z_half = mover(lambda x, zl, y, zh, c: (x, zl, y, 1 - zh, c))
core_swap = mover(lambda x, zl, y, zh, c: (x, zl, y, zh, 1 - c))
x_up = mover(lambda x, zl, y, zh, c: (x + 1, zl, y, zh, c))
x_down = mover(lambda x, zl, y, zh, c: (x - 1, zl, y, zh, c))
x_split = mover(lambda x, zl, y, zh, c: (x + 1 - 2 * c, zl, y, zh, c))


last_hop = mover(lambda x, zl, y, zh, c: (x, zl, y, 1 - zh, c) if c else (x, zl, y + 2, zh, c))


def to_column(flip):
    def rule(x, zl, y, zh, c):
        return x + y + 2 * c + flip, c, x // 2 + 2 * (zh ^ flip), x % 2, zl

    return mover(rule)


to_column_0, to_column_1 = to_column(0), to_column(1)


def after(block, *others):
    return lax.optimization_barrier((block,) + others)[0]


def dot(a, b, ca, cb):
    return lax.dot_general(a, b, (((ca,), (cb,)), ((), ())), preferred_element_type=F32)


STEP = 672
BLOCKS = ((0, 0), (1, 0), (2, 0), (3, 0), (2, 1), (3, 1))


def block_rows(j):
    return pl.ds(pl.multiple_of(j * CHIP, 16), CHIP)


def within(values, rows, cols):
    k = lax.broadcasted_iota(jnp.int32, values.shape, 0)
    l = lax.broadcasted_iota(jnp.int32, values.shape, 1)
    return jnp.where((k < rows) & (l < cols), values, 0.0).astype(BF)


def where_am_i():
    row, col = lax.axis_index("row"), lax.axis_index("col")
    return row, col, row // 2, row % 2, col // 4, (col // 2) % 2, col % 2


def slot(y, zh, dy, dz):
    return (y + dy + 4) % 4 * 2 + (zh + dz) % 2


def column_slots(dx):
    _, _, x, zl, y, zh, core = where_am_i()
    turned = x + dx - (y % 2) * 2 - zh + 16
    return [(turned - 2 * zl - o) % 4 * 2 + (y // 2 + o) % 2 for o in range(2)]


def partial_kernel(*refs):
    chip, near, near_2, mine, theirs, cols = *refs[:3], refs[3:6], refs[6:8], refs[8:11]
    self_out, pair_out, v_out, col_out, v_buf, col_buf, vsem, csem, osem = refs[11:]
    theirs = (theirs[0], near_2.at[pl.ds(6, 3)], theirs[1])
    _, _, x, zl, y, zh, core = where_am_i()
    turn = 1 - 2 * core

    def piece(src, dy, dz, n):
        rows = block_rows(slot(y, zh, dy, dz))
        return pltpu.make_async_copy(src, v_buf.at[:, rows], vsem.at[n])

    for n, (src, dy) in enumerate(((chip, 0), (near, -turn), (near_2, turn))):
        piece(src.at[pl.ds(0, 3)], dy, 0, n).start()
    for c in range(2):
        @pl.when(core == c)
        def _():
            far_e, across, _ = mine if c == 0 else theirs
            f = theirs[2] if c == 0 else mine[2]
            sources = (across, far_e.at[0], far_e.at[1], f)
            for n, (src, at) in enumerate(zip(sources, ((0, 1), (2, 0), (-1, 1), (1, 1)))):
                piece(src, *at, 3 + n).start()
    copies = []
    for i, dx in enumerate((0, -1, 1)):
        for o, j in enumerate(column_slots(dx)):
            rows = block_rows(j)
            copies.append(
                pltpu.make_async_copy(cols[i].at[o], col_buf.at[rows], csem.at[2 * i + o])
            )
    for copy in copies:
        copy.start()
    for j in column_slots(2):
        col_buf[block_rows(j), :] = jnp.zeros((CHIP, 384), BF)
    last = block_rows(slot(y, zh, 2, 1))
    for s in range(3):
        v_buf[s, last, :] = jnp.zeros((CHIP, 256), BF)
    for n in range(7):
        piece(chip.at[pl.ds(0, 3)], 0, 0, n).wait()
    for copy in copies:
        copy.wait()
    outs = [
        pltpu.make_async_copy(v_buf, v_out, osem.at[0]),
        pltpu.make_async_copy(col_buf, col_out, osem.at[1]),
    ]
    for copy in outs:
        copy.start()
    turned = col_buf[...].T
    for s in range(3):
        size = 256 if s < 2 else 384
        pair_out[:size, s * 256 : (s + 1) * 256] = dot(turned[:size], v_buf[s], 1, 0)
        self_out[s] = dot(v_buf[s], v_buf[s], 0, 0)
    for copy in outs:
        copy.wait()


def late_kernel(pair_ref, v_in, last_col, out, v_buf, col_buf, vsem, csem):
    _, _, _, _, y, zh, _ = where_am_i()
    at_cols = column_slots(2)
    copies = []
    for n in range(2):
        part = pl.ds(n * CHIP, CHIP)
        copies.append(
            pltpu.make_async_copy(v_in.at[:, block_rows(at_cols[n])], v_buf.at[:, part], vsem.at[n])
        )
        copies.append(pltpu.make_async_copy(last_col.at[n], col_buf.at[part], csem.at[n]))
    for copy in copies:
        copy.start()
    for copy in copies:
        copy.wait()
    for n in range(2):
        @pl.when(at_cols[n] == slot(y, zh, 2, 1))
        def _():
            col_buf[pl.ds(n * CHIP, CHIP), :] = jnp.zeros((CHIP, 384), BF)

    turned = col_buf[...].T
    for s in range(3):
        size = 256 if s < 2 else 384
        cut = slice(s * 256, (s + 1) * 256)
        out[:size, cut] = pair_ref[:size, cut] + dot(turned[:size], v_buf[s], 1, 0)


def final_kernel(rank_ref, *refs):
    chip, near, near_2, left_ref, self_ref, pair_ref, col_in, last_col = refs[:8]
    mine, theirs = refs[8:12], refs[12:15]
    theirs = (theirs[0], near_2.at[pl.ds(6, 3)], *theirs[1:])
    off, diag = refs[15:17]
    v_buf, u_buf, col_buf, zero, stage, wide, vsem, usem, csem, zsem, osem, dsem = refs[17:]
    row, col, x, zl, y, zh, core = where_am_i()
    turn = 1 - 2 * core

    def piece(src, dy, dz, n):
        rows = block_rows(slot(y, zh, dy, dz))
        return pltpu.make_async_copy(src, u_buf.at[:, rows], usem.at[n])

    at_last = slot(y, zh, 2, 1)
    at_cols = column_slots(2)

    def col_copy(src):
        return pltpu.make_async_copy(src, col_buf, csem)

    for n in range(2):
        @pl.when(at_cols[n] == at_last)
        def _():
            col_copy(last_col.at[n]).start()

    @pl.when((at_cols[0] != at_last) & (at_cols[1] != at_last))
    def _():
        col_copy(col_in.at[block_rows(at_last)]).start()

    for n, (src, dy) in enumerate(((chip, 0), (near, -turn), (near_2, turn))):
        piece(src.at[pl.ds(3, 3)], dy, 0, n).start()
    for c in range(2):
        @pl.when(core == c)
        def _():
            pltpu.make_async_copy((mine if c == 0 else theirs)[3], v_buf, vsem).start()
            far_e, across, _, g = theirs if c == 0 else mine
            f = mine[2] if c == 0 else theirs[2]
            sources = (across, far_e.at[0], far_e.at[1], f, g)
            for n, (src, at) in enumerate(zip(sources, ((0, 1), (2, 0), (1, 1), (-1, 1), (2, 1)))):
                piece(src, *at, 3 + n).start()

    zero[...] = jnp.zeros_like(zero)
    zeros = [pltpu.make_async_copy(zero, off.at[p, 1], zsem.at[p]) for p in range(2)]
    for copy in zeros:
        copy.start()
    for n in (4, 5):
        stage[n, :, 128:] = jnp.zeros((NB, 128), BF)
    row_ranks = [rank_ref[row * 4 + p] for p in range(4)]
    col_ranks = [rank_ref[col % 8 * 4 + 2 * q + col // 8] for q in range(2)]

    def kept(p, q):
        return jnp.where(p * 8 + row > q * 16 + col, row_ranks[p], 0)

    pltpu.make_async_copy(mine[3], v_buf, vsem).wait()
    col_copy(last_col.at[0]).wait()
    turned = col_buf[...].T

    def whole_pair(s, rows):
        total = pair_ref[:rows, s * 256 : (s + 1) * 256] + dot(turned[:rows], v_buf[s], 1, 0)
        return total.T

    ready = [[within(whole_pair(p, 256), kept(p, 0), col_ranks[0])] for p in range(2)]
    both = whole_pair(2, 384)
    for p in range(2, 4):
        rows = slice((p - 2) * 128, (p - 1) * 128)
        cuts = (slice(0, 256), slice(256, 384))
        ready.append(
            [within(both[rows, cut], kept(p, q), col_ranks[q]) for q, cut in enumerate(cuts)]
        )
    inners = []
    for p in range(4):
        s = min(p, 2)
        cut = slice(0, 256) if p < 2 else slice((p - 2) * 128, (p - 1) * 128)
        if p < 3:
            own = self_ref[s] + dot(v_buf[s], v_buf[s], 0, 0)
        square = within(own[cut, cut], row_ranks[p], row_ranks[p])
        inners.append(dot(left_ref[p, :, : cut.stop - cut.start], square, 1, 0).astype(BF))
    for n in range(8):
        piece(chip.at[pl.ds(3, 3)], 0, 0, n).wait()

    out_copies = []

    def send(n):
        p, q = BLOCKS[n]
        out_copies.append(pltpu.make_async_copy(stage.at[n], off.at[p, q], osem.at[n]))
        out_copies[-1].start()

    for p in range(2):
        stage[p] = dot(u_buf[p], ready[p][0], 1, 0).astype(BF)
        send(p)
    for p in range(2, 4):
        both = jnp.concatenate(ready[p], axis=1)
        part = u_buf[2, :, (p - 2) * 128 : (p - 1) * 128]
        both = dot(part, both, 1, 0).astype(BF)
        stage[p] = both[:, :256]
        send(p)
        stage[p + 2, :, :128] = both[:, 256:]
        send(p + 2)

    diag_copies = []
    for p in range(4):
        s = min(p, 2)
        cut = slice(0, 256) if p < 2 else slice((p - 2) * 128, (p - 1) * 128)
        wide[p] = dot(inners[p], u_buf[s, :, cut], 1, 1).astype(BF)
        diag_copies.append(pltpu.make_async_copy(wide.at[p], diag.at[p], dsem.at[p]))
        diag_copies[-1].start()
    for copy in zeros + out_copies + diag_copies:
        copy.wait()


SMEM = pl.BlockSpec(memory_space=pltpu.SMEM)
VMEM = pl.BlockSpec(memory_space=pltpu.VMEM)
ANY = pl.BlockSpec(memory_space=pl.ANY)


def per_device(left_factors, right_factors, ranks):
    col = lax.axis_index("col")
    zh, core = (col // 2) % 2, col % 2
    first = core == 0
    shape, params = jax.ShapeDtypeStruct, pltpu.CompilerParams(vmem_limit_bytes=LIMIT)
    dma = pltpu.SemaphoreType.DMA
    def packed(tiles):
        return jnp.stack(
            [tiles[0], tiles[1], jnp.concatenate([tiles[2, :, :128], tiles[3, :, :128]], axis=1)]
        )

    def chip_block(own, other):
        low, high = jnp.where(first, own, other), jnp.where(first, other, own)
        return jnp.concatenate([packed(low), packed(high)], axis=1)

    other_v, other_u = core_swap(right_factors), core_swap(left_factors)
    chip = jnp.concatenate(
        [chip_block(right_factors, other_v), chip_block(left_factors, other_u)]
    )

    def column_block(a):
        near = jnp.where(a == 0, chip[0], chip[1])
        far = jnp.where(a == 0, chip[2, :, :128], chip[2, :, 128:])
        return jnp.concatenate([near, far], axis=1)

    role = jnp.where(first, chip[:3], chip[3:])
    chip, role, block0, block1 = lax.optimization_barrier(
        (chip, role, column_block(zh), column_block(1 - zh))
    )
    near, across = y_split(chip), z_half(role)
    got = jnp.stack([to_column_0(block0), to_column_1(block1)])
    near, across, got = lax.optimization_barrier((near, across, got))
    far_e = y_split(jnp.stack([jnp.where(first, near[:3], near[3:]), across]))
    f = z_half(jnp.where(first, near[3:], near[:3]))
    near_2 = core_swap(jnp.concatenate([near, across]))
    left_col, right_col = x_up(got), x_down(got)
    far_e, f, left_col, right_col = lax.optimization_barrier((far_e, f, left_col, right_col))
    g = last_hop(jnp.where(first, across, far_e[0]))
    last_col = x_split(jnp.where(first, left_col, right_col))
    far_e2, f_2 = core_swap(far_e), core_swap(f)
    selfpart, pairpart, v_full, col_full = pl.pallas_call(
        partial_kernel,
        out_shape=(
            shape((3, 256, 256), F32), shape((384, 768), F32),
            shape((3, NB, 256), BF), shape((NB, 384), BF),
        ),
        in_specs=[ANY] * 11,
        out_specs=(VMEM, VMEM, ANY, ANY),
        scratch_shapes=[
            pltpu.VMEM((3, NB, 256), BF), pltpu.VMEM((NB, 384), BF), dma((7,)), dma((6,)), dma((2,)),
        ],
        compiler_params=params,
        cost_estimate=pl.CostEstimate(
            flops=4_000_000_000, bytes_accessed=15_000_000, transcendentals=0
        ),
    )(chip, near, near_2, far_e, across, f, far_e2, f_2, got, left_col, right_col)
    g_2 = core_swap(after(g, selfpart))
    pairpart = pl.pallas_call(
        late_kernel,
        out_shape=shape((384, 768), F32),
        in_specs=[VMEM, ANY, ANY],
        out_specs=VMEM,
        scratch_shapes=[
            pltpu.VMEM((3, 2 * CHIP, 256), BF), pltpu.VMEM((2 * CHIP, 384), BF), dma((2,)), dma((2,)),
        ],
        compiler_params=params,
        cost_estimate=pl.CostEstimate(
            flops=800_000_000, bytes_accessed=4_000_000, transcendentals=0
        ),
    )(pairpart, v_full, last_col)
    return pl.pallas_call(
        final_kernel,
        out_shape=(shape((4, 2, NB, 256), BF), shape((4, PTS, NB), BF)),
        in_specs=[SMEM] + [ANY] * 3 + [VMEM] * 3 + [ANY] * 9,
        out_specs=(ANY, ANY),
        scratch_shapes=[
            pltpu.VMEM((3, CHIP, 256), BF),
            pltpu.VMEM((3, NB, 256), BF),
            pltpu.VMEM((CHIP, 384), BF),
            pltpu.VMEM((NB, 256), BF),
            pltpu.VMEM((6, NB, 256), BF),
            pltpu.VMEM((4, PTS, NB), BF),
            dma, dma((8,)), dma, dma((2,)), dma((6,)), dma((4,)),
        ],
        compiler_params=params,
        cost_estimate=pl.CostEstimate(
            flops=6_000_000_000, bytes_accessed=25_000_000, transcendentals=0
        ),
    )(
        ranks, chip, near, near_2, left_factors, selfpart, pairpart, col_full, last_col,
        far_e, across, f, g, far_e2, f_2, g_2,
    )


def solution(mesh):
    in_specs = (P("row", "col", None), P("row", "col", None), P())
    out_specs = (P("row", "col", None, None), P("row", "col", None))
    return jax.shard_map(
        per_device, mesh=mesh, in_specs=in_specs, out_specs=out_specs, check_vma=False
    )
```

profile of v0, /device:TPU:1, one launch (start us, length us, event | category | flops | bytes accessed | tf_op | source)
XLA Modules:
  0.0 74.0 jit_solution(12357023768326071014)
XLA Ops:
  0.6 1.5 %collective-permute-start = (bf16[4,168,256]{2,1,0:T(8,128)(2,1)}, bf16[4,168,256]{2,1,0:T(8,128)(2,1)S(1)}, u32[]{:S(2)}, u32[]{:S(2)}) collective-permute-start(bf16[4,168,256]{2,1,0:T(8,128)(2,1)} %param.4), channel_id=1, source_target_pairs={{0,1},{1,0},{2,3},{3,2},{4,5},{5,4},{6,7},{7,6},{8,9},{9,8},{10,11... | collective-permute-start | bytes 1032200 | tf_op jit(solution)/shard_map/ppermute | solution.py:22
  2.2 1.4 %collective-permute-done = bf16[4,168,256]{2,1,0:T(8,128)(2,1)S(1)} collective-permute-done((bf16[4,168,256]{2,1,0:T(8,128)(2,1)}, bf16[4,168,256]{2,1,0:T(8,128)(2,1)S(1)}, u32[]{:S(2)}, u32[]{:S(2)}) %collective-permute-start) | collective-permute-done | bytes 344096 | tf_op jit(solution)/shard_map/ppermute | solution.py:22
  3.6 0.5 collective-permute-done.1
  4.1 1.2 %broadcast_select_fusion.3 = (bf16[4,168,256]{2,1,0:T(8,128)(2,1)S(1)}, bf16[4,168,256]{2,1,0:T(8,128)(2,1)S(1)}, bf16[4,168,256]{2,1,0:T(8,128)(2,1)S(1)}, bf16[4,168,256]{2,1,0:T(8,128)(2,1)S(1)}) fusion(bf16[4,168,256]{2,1,0:T(8,128)(2,1)} %refs_3_.1, bf16[4,168,256]{2,1,0:T(8,128)(2,1)S(1)} %collective-permute-done.1, pred[]{:T(512)S(6)} %eq.14, ...), kind=kLoop, calls=%fused_computation.11 | loop fusion | flops 688128 | bytes 2752513 | tf_op jit(solution)/shard_map/jit(_where)/select_n | solution.py:289
  5.6 0.2 maximum_maximum_fusion.1
  5.9 2.9 %collective-permute-start.2 = (bf16[6,336,256]{2,1,0:T(8,128)(2,1)S(1)}, bf16[6,336,256]{2,1,0:T(8,128)(2,1)S(1)}, u32[]{:S(2)}, u32[]{:S(2)}) collective-permute-start(bf16[6,336,256]{2,1,0:T(8,128)(2,1)S(1)} %maximum_maximum_fusion.refs_0_), channel_id=1, source_target_pairs={{0,4},{1,13},{2,6},{3,15},{4,8},{5,1},{6,10},{7,3},{8,12},{9,5},{1... | collective-permute-start | bytes 3096584 | tf_op jit(solution)/shard_map/ppermute | solution.py:22
  8.8 3.6 %collective-permute-start.3 = (bf16[3,336,256]{2,1,0:T(8,128)(2,1)S(1)}, bf16[3,336,256]{2,1,0:T(8,128)(2,1)S(1)}, u32[]{:S(2)}, u32[]{:S(2)}) collective-permute-start(bf16[3,336,256]{2,1,0:T(8,128)(2,1)S(1)} %get-tuple-element.19), channel_id=1, source_target_pairs={{0,2},{1,3},{2,0},{3,1},{4,6},{5,7},{6,4},{7,5},{8,10},{9,11},{10,... | collective-permute-start | bytes 1548296 | tf_op jit(solution)/shard_map/ppermute | solution.py:22
  12.4 4.5 %collective-permute-start.4 = (bf16[336,384]{1,0:T(8,128)(2,1)S(1)}, bf16[336,384]{1,0:T(8,128)(2,1)S(1)}, u32[]{:S(2)}, u32[]{:S(2)}) collective-permute-start(bf16[336,384]{1,0:T(8,128)(2,1)S(1)} %pad_maximum_fusion.3), channel_id=1, source_target_pairs={{0,0},{1,80},{2,8},{3,88},{4,32},{5,112},{6,40},{7,120},{8,64},{9,... | collective-permute-start | bytes 774152 | tf_op jit(solution)/shard_map/ppermute | solution.py:22
  16.9 4.0 %collective-permute-start.5 = (bf16[336,384]{1,0:T(8,128)(2,1)S(1)}, bf16[336,384]{1,0:T(8,128)(2,1)S(1)}, u32[]{:S(2)}, u32[]{:S(2)}) collective-permute-start(bf16[336,384]{1,0:T(8,128)(2,1)S(1)} %pad_maximum_fusion.4), channel_id=1, source_target_pairs={{0,40},{1,120},{2,32},{3,112},{4,72},{5,24},{6,64},{7,16},{8,104},... | collective-permute-start | bytes 774152 | tf_op jit(solution)/shard_map/ppermute | solution.py:22
  20.9 12.2 %collective-permute-done.4 = bf16[336,384]{1,0:T(8,128)(2,1)S(1)} collective-permute-done((bf16[336,384]{1,0:T(8,128)(2,1)S(1)}, bf16[336,384]{1,0:T(8,128)(2,1)S(1)}, u32[]{:S(2)}, u32[]{:S(2)}) %collective-permute-start.4) | collective-permute-done | bytes 258080 | tf_op jit(solution)/shard_map/ppermute | solution.py:22
  33.5 1.5 %collective-permute-start.10 = (bf16[2,336,384]{2,1,0:T(8,128)(2,1)S(1)}, bf16[2,336,384]{2,1,0:T(8,128)(2,1)S(1)}, u32[]{:S(2)}, u32[]{:S(2)}) collective-permute-start(bf16[2,336,384]{2,1,0:T(8,128)(2,1)S(1)} %pad_maximum_fusion.2.refs_8_), channel_id=1, source_target_pairs={{0,96},{1,97},{2,98},{3,99},{4,100},{5,101},{6,102},{7,103},{8,104... | collective-permute-start | bytes 1548296 | tf_op jit(solution)/shard_map/ppermute | solution.py:22
  35.0 1.4 %collective-permute-start.8 = (bf16[3,336,256]{2,1,0:T(8,128)(2,1)S(1)}, bf16[3,336,256]{2,1,0:T(8,128)(2,1)S(1)}, u32[]{:S(2)}, u32[]{:S(2)}) collective-permute-start(bf16[3,336,256]{2,1,0:T(8,128)(2,1)S(1)} %get-tuple-element.34), channel_id=1, source_target_pairs={{0,2},{1,3},{2,0},{3,1},{4,6},{5,7},{6,4},{7,5},{8,10},{9,11},{10,... | collective-permute-start | bytes 1548296 | tf_op jit(solution)/shard_map/ppermute | solution.py:22
  36.4 0.1 pad_maximum_fusion
  36.6 2.1 %collective-permute-start.6 = (bf16[9,336,256]{2,1,0:T(8,128)(2,1)S(1)}, bf16[9,336,256]{2,1,0:T(8,128)(2,1)S(1)}, u32[]{:S(2)}, u32[]{:S(2)}) collective-permute-start(bf16[9,336,256]{2,1,0:T(8,128)(2,1)S(1)} %pad_maximum_fusion), channel_id=1, source_target_pairs={{0,1},{1,0},{2,3},{3,2},{4,5},{5,4},{6,7},{7,6},{8,9},{9,8},{10,11... | collective-permute-start | bytes 4644872 | tf_op jit(solution)/shard_map/ppermute | solution.py:22
  38.6 8.6 %collective-permute-done.10.refs_10_ = bf16[2,336,384]{2,1,0:T(8,128)(2,1)S(1)} collective-permute-done((bf16[2,336,384]{2,1,0:T(8,128)(2,1)S(1)}, bf16[2,336,384]{2,1,0:T(8,128)(2,1)S(1)}, u32[]{:S(2)}, u32[]{:S(2)}) %collective-permute-start.10) | collective-permute-done | bytes 516128 | tf_op jit(solution)/shard_map/ppermute | solution.py:22
  47.2 1.9 %collective-permute-done.9.refs_9_ = bf16[2,336,384]{2,1,0:T(8,128)(2,1)S(1)} collective-permute-done((bf16[2,336,384]{2,1,0:T(8,128)(2,1)S(1)}, bf16[2,336,384]{2,1,0:T(8,128)(2,1)S(1)}, u32[]{:S(2)}, u32[]{:S(2)}) %collective-permute-start.9) | collective-permute-done | bytes 516128 | tf_op jit(solution)/shard_map/ppermute | solution.py:22
  49.2 0.3 collective-permute-done.8.refs_5_.refs_10_
  49.5 1.2 %collective-permute-start.11 = (bf16[2,3,336,256]{3,2,1,0:T(8,128)(2,1)S(1)}, bf16[2,3,336,256]{3,2,1,0:T(8,128)(2,1)S(1)}, u32[]{:S(2)}, u32[]{:S(2)}) collective-permute-start(bf16[2,3,336,256]{3,2,1,0:T(8,128)(2,1)S(1)} %collective-permute-done.7.refs_3_.refs_8_), channel_id=1, source_target_pairs={{0,1},{1,0},{2,3},{3,2},{4,5},{5,4},{6,7},{7,6},{8,9},{9,8},{10,11... | collective-permute-start | bytes 3096584 | tf_op jit(solution)/shard_map/ppermute | solution.py:22
  50.7 1.5 %collective-permute-start.14 = (bf16[3,336,256]{2,1,0:T(8,128)(2,1)S(1)}, bf16[3,336,256]{2,1,0:T(8,128)(2,1)S(1)}, u32[]{:S(2)}, u32[]{:S(2)}) collective-permute-start(bf16[3,336,256]{2,1,0:T(8,128)(2,1)S(1)} %bitcast_select_fusion), channel_id=1, source_target_pairs={{0,8},{1,3},{2,10},{3,1},{4,12},{5,7},{6,14},{7,5},{8,0},{9,11},{1... | collective-permute-start | bytes 1548296 | tf_op jit(solution)/shard_map/ppermute | solution.py:22
  52.3 2.7 %collective-permute-start.13 = (bf16[2,336,384]{2,1,0:T(8,128)(2,1)S(1)}, bf16[2,336,384]{2,1,0:T(8,128)(2,1)S(1)}, u32[]{:S(2)}, u32[]{:S(2)}) collective-permute-start(bf16[2,336,384]{2,1,0:T(8,128)(2,1)S(1)} %broadcast_select_fusion), channel_id=1, source_target_pairs={{0,32},{1,97},{2,34},{3,99},{4,36},{5,101},{6,38},{7,103},{8,40},{... | collective-permute-start | bytes 1548296 | tf_op jit(solution)/shard_map/ppermute | solution.py:22
  55.1 7.2 %shard_map.50 = (f32[3,256,256]{2,1,0:T(8,128)S(1)}, f32[384,768]{1,0:T(8,128)S(1)}, bf16[3,2688,256]{2,1,0:T(8,128)(2,1)S(1)}, bf16[2688,384]{1,0:T(8,128)(2,1)S(1)}) custom-call(bf16[6,336,256]{2,1,0:T(8,128)(2,1)S(1)} %maximum_maximum_fusion.refs_0_, bf16[6,336,256]{2,1,0:T(8,128)(2,1)S(1)} %collective-permute-done.2.refs_1_, ...), custom_call_target="tpu_custom_call" | custom-call | flops 4000000000 | bytes 15000000 | tf_op jit(solution)/shard_map/pallas_call | solution.py:317
  62.4 1.5 %shard_map.51.refs_5_ = f32[384,768]{1,0:T(8,128)S(1)} custom-call(f32[384,768]{1,0:T(8,128)S(1)} %get-tuple-element.30.pair_ref, bf16[3,2688,256]{2,1,0:T(8,128)(2,1)S(1)} %get-tuple-element.31.v_in, bf16[2,336,384]{2,1,0:T(8,128)(2,1)S(1)} %collective-permute-done.13.last_col.refs_7_), custom_call_target="tpu_custom_call" | custom-call | flops 800000000 | bytes 4000000 | tf_op jit(solution)/shard_map/pallas_call | solution.py:334
  64.0 0.3 collective-permute-done.15.refs_14_
  64.3 9.6 %shard_map.52 = (bf16[4,2,2688,256]{3,2,1,0:T(8,128)(2,1)}, bf16[4,168,2688]{2,1,0:T(8,128)(2,1)}) custom-call(s32[32]{0:T(128)S(1)} %copy-done.1, bf16[6,336,256]{2,1,0:T(8,128)(2,1)S(1)} %maximum_maximum_fusion.refs_0_, bf16[6,336,256]{2,1,0:T(8,128)(2,1)S(1)} %collective-permute-done.2.refs_1_, bf16[9,336,256]{2,1,0:T(8,128)(2,1)S(1)} %collective-permute-done.6.refs_2_, ...), custom_call_target="tpu_custom_call" | custom-call | flops 6000000000 | bytes 25000000 | tf_op jit(solution)/shard_map/pallas_call | solution.py:347
  (40 shorter events, 1.0 us)
Async XLA Ops:
  0.6 3.0 %collective-permute-start = (bf16[4,168,256]{2,1,0:T(8,128)(2,1)}, bf16[4,168,256]{2,1,0:T(8,128)(2,1)S(1)}, u32[]{:S(2)}, u32[]{:S(2)}) collective-permute-start(bf16[4,168,256]{2,1,0:T(8,128)(2,1)} %param.4), channel_id=1, source_target_pairs={{0,1},{1,0},{2,3},{3,2},{4,5},{5,4},{6,7},{7,6},{8,9},{9,8},{10,11... | collective-permute-start | bytes 1032200 | tf_op jit(solution)/shard_map/ppermute | solution.py:22
  2.1 2.0 %collective-permute-start.1 = (bf16[4,168,256]{2,1,0:T(8,128)(2,1)}, bf16[4,168,256]{2,1,0:T(8,128)(2,1)S(1)}, u32[]{:S(2)}, u32[]{:S(2)}) collective-permute-start(bf16[4,168,256]{2,1,0:T(8,128)(2,1)} %refs_3_.1), channel_id=1, source_target_pairs={{0,1},{1,0},{2,3},{3,2},{4,5},{5,4},{6,7},{7,6},{8,9},{9,8},{10,11... | collective-permute-start | bytes 1032200 | tf_op jit(solution)/shard_map/ppermute | solution.py:22
  5.9 27.2 %collective-permute-start.2 = (bf16[6,336,256]{2,1,0:T(8,128)(2,1)S(1)}, bf16[6,336,256]{2,1,0:T(8,128)(2,1)S(1)}, u32[]{:S(2)}, u32[]{:S(2)}) collective-permute-start(bf16[6,336,256]{2,1,0:T(8,128)(2,1)S(1)} %maximum_maximum_fusion.refs_0_), channel_id=1, source_target_pairs={{0,4},{1,13},{2,6},{3,15},{4,8},{5,1},{6,10},{7,3},{8,12},{9,5},{1... | collective-permute-start | bytes 3096584 | tf_op jit(solution)/shard_map/ppermute | solution.py:22
  8.8 24.3 %collective-permute-start.3 = (bf16[3,336,256]{2,1,0:T(8,128)(2,1)S(1)}, bf16[3,336,256]{2,1,0:T(8,128)(2,1)S(1)}, u32[]{:S(2)}, u32[]{:S(2)}) collective-permute-start(bf16[3,336,256]{2,1,0:T(8,128)(2,1)S(1)} %get-tuple-element.19), channel_id=1, source_target_pairs={{0,2},{1,3},{2,0},{3,1},{4,6},{5,7},{6,4},{7,5},{8,10},{9,11},{10,... | collective-permute-start | bytes 1548296 | tf_op jit(solution)/shard_map/ppermute | solution.py:22
  12.4 20.7 %collective-permute-start.4 = (bf16[336,384]{1,0:T(8,128)(2,1)S(1)}, bf16[336,384]{1,0:T(8,128)(2,1)S(1)}, u32[]{:S(2)}, u32[]{:S(2)}) collective-permute-start(bf16[336,384]{1,0:T(8,128)(2,1)S(1)} %pad_maximum_fusion.3), channel_id=1, source_target_pairs={{0,0},{1,80},{2,8},{3,88},{4,32},{5,112},{6,40},{7,120},{8,64},{9,... | collective-permute-start | bytes 774152 | tf_op jit(solution)/shard_map/ppermute | solution.py:22
  16.9 16.2 %collective-permute-start.5 = (bf16[336,384]{1,0:T(8,128)(2,1)S(1)}, bf16[336,384]{1,0:T(8,128)(2,1)S(1)}, u32[]{:S(2)}, u32[]{:S(2)}) collective-permute-start(bf16[336,384]{1,0:T(8,128)(2,1)S(1)} %pad_maximum_fusion.4), channel_id=1, source_target_pairs={{0,40},{1,120},{2,32},{3,112},{4,72},{5,24},{6,64},{7,16},{8,104},... | collective-permute-start | bytes 774152 | tf_op jit(solution)/shard_map/ppermute | solution.py:22
  33.4 16.1 %collective-permute-start.7 = (bf16[2,3,336,256]{3,2,1,0:T(8,128)(2,1)S(1)}, bf16[2,3,336,256]{3,2,1,0:T(8,128)(2,1)S(1)}, u32[]{:S(2)}, u32[]{:S(2)}) collective-permute-start(bf16[2,3,336,256]{3,2,1,0:T(8,128)(2,1)S(1)} %pad_maximum_fusion.1), channel_id=1, source_target_pairs={{0,4},{1,13},{2,6},{3,15},{4,8},{5,1},{6,10},{7,3},{8,12},{9,5},{1... | collective-permute-start | bytes 3096584 | tf_op jit(solution)/shard_map/ppermute | solution.py:22
  33.5 13.8 %collective-permute-start.10 = (bf16[2,336,384]{2,1,0:T(8,128)(2,1)S(1)}, bf16[2,336,384]{2,1,0:T(8,128)(2,1)S(1)}, u32[]{:S(2)}, u32[]{:S(2)}) collective-permute-start(bf16[2,336,384]{2,1,0:T(8,128)(2,1)S(1)} %pad_maximum_fusion.2.refs_8_), channel_id=1, source_target_pairs={{0,96},{1,97},{2,98},{3,99},{4,100},{5,101},{6,102},{7,103},{8,104... | collective-permute-start | bytes 1548296 | tf_op jit(solution)/shard_map/ppermute | solution.py:22
  35.0 14.2 %collective-permute-start.9 = (bf16[2,336,384]{2,1,0:T(8,128)(2,1)S(1)}, bf16[2,336,384]{2,1,0:T(8,128)(2,1)S(1)}, u32[]{:S(2)}, u32[]{:S(2)}) collective-permute-start(bf16[2,336,384]{2,1,0:T(8,128)(2,1)S(1)} %pad_maximum_fusion.2.refs_8_), channel_id=1, source_target_pairs={{0,32},{1,33},{2,34},{3,35},{4,36},{5,37},{6,38},{7,39},{8,40},{9,... | collective-permute-start | bytes 1548296 | tf_op jit(solution)/shard_map/ppermute | solution.py:22
  35.0 14.5 %collective-permute-start.8 = (bf16[3,336,256]{2,1,0:T(8,128)(2,1)S(1)}, bf16[3,336,256]{2,1,0:T(8,128)(2,1)S(1)}, u32[]{:S(2)}, u32[]{:S(2)}) collective-permute-start(bf16[3,336,256]{2,1,0:T(8,128)(2,1)S(1)} %get-tuple-element.34), channel_id=1, source_target_pairs={{0,2},{1,3},{2,0},{3,1},{4,6},{5,7},{6,4},{7,5},{8,10},{9,11},{10,... | collective-permute-start | bytes 1548296 | tf_op jit(solution)/shard_map/ppermute | solution.py:22
  36.6 18.5 %collective-permute-start.6 = (bf16[9,336,256]{2,1,0:T(8,128)(2,1)S(1)}, bf16[9,336,256]{2,1,0:T(8,128)(2,1)S(1)}, u32[]{:S(2)}, u32[]{:S(2)}) collective-permute-start(bf16[9,336,256]{2,1,0:T(8,128)(2,1)S(1)} %pad_maximum_fusion), channel_id=1, source_target_pairs={{0,1},{1,0},{2,3},{3,2},{4,5},{5,4},{6,7},{7,6},{8,9},{9,8},{10,11... | collective-permute-start | bytes 4644872 | tf_op jit(solution)/shard_map/ppermute | solution.py:22
  49.5 5.6 %collective-permute-start.11 = (bf16[2,3,336,256]{3,2,1,0:T(8,128)(2,1)S(1)}, bf16[2,3,336,256]{3,2,1,0:T(8,128)(2,1)S(1)}, u32[]{:S(2)}, u32[]{:S(2)}) collective-permute-start(bf16[2,3,336,256]{3,2,1,0:T(8,128)(2,1)S(1)} %collective-permute-done.7.refs_3_.refs_8_), channel_id=1, source_target_pairs={{0,1},{1,0},{2,3},{3,2},{4,5},{5,4},{6,7},{7,6},{8,9},{9,8},{10,11... | collective-permute-start | bytes 3096584 | tf_op jit(solution)/shard_map/ppermute | solution.py:22
  50.7 4.4 %collective-permute-start.12 = (bf16[3,336,256]{2,1,0:T(8,128)(2,1)S(1)}, bf16[3,336,256]{2,1,0:T(8,128)(2,1)S(1)}, u32[]{:S(2)}, u32[]{:S(2)}) collective-permute-start(bf16[3,336,256]{2,1,0:T(8,128)(2,1)S(1)} %collective-permute-done.8.refs_5_.refs_10_), channel_id=1, source_target_pairs={{0,1},{1,0},{2,3},{3,2},{4,5},{5,4},{6,7},{7,6},{8,9},{9,8},{10,11... | collective-permute-start | bytes 1548296 | tf_op jit(solution)/shard_map/ppermute | solution.py:22
  50.7 11.6 %collective-permute-start.14 = (bf16[3,336,256]{2,1,0:T(8,128)(2,1)S(1)}, bf16[3,336,256]{2,1,0:T(8,128)(2,1)S(1)}, u32[]{:S(2)}, u32[]{:S(2)}) collective-permute-start(bf16[3,336,256]{2,1,0:T(8,128)(2,1)S(1)} %bitcast_select_fusion), channel_id=1, source_target_pairs={{0,8},{1,3},{2,10},{3,1},{4,12},{5,7},{6,14},{7,5},{8,0},{9,11},{1... | collective-permute-start | bytes 1548296 | tf_op jit(solution)/shard_map/ppermute | solution.py:22
  52.3 10.1 %collective-permute-start.13 = (bf16[2,336,384]{2,1,0:T(8,128)(2,1)S(1)}, bf16[2,336,384]{2,1,0:T(8,128)(2,1)S(1)}, u32[]{:S(2)}, u32[]{:S(2)}) collective-permute-start(bf16[2,336,384]{2,1,0:T(8,128)(2,1)S(1)} %broadcast_select_fusion), channel_id=1, source_target_pairs={{0,32},{1,97},{2,34},{3,99},{4,36},{5,101},{6,38},{7,103},{8,40},{... | collective-permute-start | bytes 1548296 | tf_op jit(solution)/shard_map/ppermute | solution.py:22
  62.3 2.0 %collective-permute-start.15 = (bf16[3,336,256]{2,1,0:T(8,128)(2,1)S(1)}, bf16[3,336,256]{2,1,0:T(8,128)(2,1)S(1)}, u32[]{:S(2)}, u32[]{:S(2)}) collective-permute-start(bf16[3,336,256]{2,1,0:T(8,128)(2,1)S(1)} %collective-permute-done.14.refs_11_), channel_id=1, source_target_pairs={{0,1},{1,0},{2,3},{3,2},{4,5},{5,4},{6,7},{7,6},{8,9},{9,8},{10,11... | collective-permute-start | bytes 1548296 | tf_op jit(solution)/shard_map/ppermute | solution.py:22
  62.4 1.9 %copy-start = (bf16[4,168,256]{2,1,0:T(8,128)(2,1)S(1)}, bf16[4,168,256]{2,1,0:T(8,128)(2,1)}, u32[]{:S(2)}) copy-start(bf16[4,168,256]{2,1,0:T(8,128)(2,1)} %refs_3_.1) | copy-start | bytes 1032196
  62.4 1.9 %copy-start.1 = (s32[32]{0:T(128)S(1)}, s32[32]{0:T(128)}, u32[]{:S(2)}) copy-start(s32[32]{0:T(128)} %rank_ref.1) | copy-start | bytes 388
where the time goes:
time: 74.2 us; the launch traced here: 74 us
  starting transfers between devices  27.2 us (37%)
  waiting for transfers between devices  25.3 us (34%)
  Pallas kernels  18.4 us (25%)
  other arithmetic  2.12 us (3%)
  between operations  1.06 us (1%)
    ppermute x16, starting transfers between devices, mover(): return lambda block: lax.ppermute(block, AXES, pairs)  27.2 us
    ppermute x16, waiting for transfers between devices, mover(): return lambda block: lax.ppermute(block, AXES, pairs)  25.3 us
    pallas_call x1, Pallas kernels, per_device(): pl.pallas_call(final_kernel, out_shape=(shape((4, 2, NB, 256), BF), shape...  9.58 us
    pallas_call x1, Pallas kernels, per_device(): pl.pallas_call(partial_kernel, out_shape=(shape((3, 256, 256), F32), shap...  7.24 us
    pallas_call x1, Pallas kernels, per_device(): pl.pallas_call(late_kernel, out_shape=shape((384, 768), F32), in_specs=[V...  1.54 us
  transfers between devices with their start and end apart: 16, of which 7 were waited for; matrix products, arithmetic and copies ran while one was open for 0% of the time, Pallas kernels for 12%

commit v1 on v0

--- a/solution.py
+++ b/solution.py
@@ -217,16 +217,15 @@
     turned = col_buf[...].T
 
     def whole_pair(s, rows):
-        total = pair_ref[:rows, s * 256 : (s + 1) * 256] + dot(turned[:rows], v_buf[s], 1, 0)
-        return total.T
-
-    ready = [[within(whole_pair(p, 256), kept(p, 0), col_ranks[0])] for p in range(2)]
+        return pair_ref[:rows, s * 256 : (s + 1) * 256] + dot(turned[:rows], v_buf[s], 1, 0)
+
+    ready = [[within(whole_pair(p, 256), col_ranks[0], kept(p, 0))] for p in range(2)]
     both = whole_pair(2, 384)
     for p in range(2, 4):
         rows = slice((p - 2) * 128, (p - 1) * 128)
         cuts = (slice(0, 256), slice(256, 384))
         ready.append(
-            [within(both[rows, cut], kept(p, q), col_ranks[q]) for q, cut in enumerate(cuts)]
+            [within(both[cut, rows], col_ranks[q], kept(p, q)) for q, cut in enumerate(cuts)]
         )
     inners = []
     for p in range(4):
@@ -247,12 +246,12 @@
         out_copies[-1].start()
 
     for p in range(2):
-        stage[p] = dot(u_buf[p], ready[p][0], 1, 0).astype(BF)
+        stage[p] = dot(u_buf[p], ready[p][0], 1, 1).astype(BF)
         send(p)
     for p in range(2, 4):
-        both = jnp.concatenate(ready[p], axis=1)
+        both = jnp.concatenate(ready[p], axis=0)
         part = u_buf[2, :, (p - 2) * 128 : (p - 1) * 128]
-        both = dot(part, both, 1, 0).astype(BF)
+        both = dot(part, both, 1, 1).astype(BF)
         stage[p] = both[:, :256]
         send(p)
         stage[p + 2, :, :128] = both[:, 256:]

time: 74.2 us -> 74.3 us (level)
  no operation moved by 1% of the time
where the time goes in v1:
time: 74.3 us; the launch traced here: 74.1 us
  starting transfers between devices  27.2 us (37%)
  waiting for transfers between devices  25.3 us (34%)
  Pallas kernels  18.4 us (25%)
  other arithmetic  2.12 us (3%)
  between operations  1.06 us (1%)
    ppermute x16, starting transfers between devices, mover(): return lambda block: lax.ppermute(block, AXES, pairs)  27.2 us
    ppermute x16, waiting for transfers between devices, mover(): return lambda block: lax.ppermute(block, AXES, pairs)  25.3 us
    pallas_call x1, Pallas kernels, per_device(): pl.pallas_call(final_kernel, out_shape=(shape((4, 2, NB, 256), BF), shape...  9.64 us
    pallas_call x1, Pallas kernels, per_device(): pl.pallas_call(partial_kernel, out_shape=(shape((3, 256, 256), F32), shap...  7.24 us
    pallas_call x1, Pallas kernels, per_device(): pl.pallas_call(late_kernel, out_shape=shape((384, 768), F32), in_specs=[V...  1.54 us
  transfers between devices with their start and end apart: 16, of which 7 were waited for; matrix products, arithmetic and copies ran while one was open for 0% of the time, Pallas kernels for 12%

profile of v1, /device:TPU:1, one launch (start us, length us, event | category | flops | bytes accessed | tf_op | source)
XLA Modules:
  0.0 74.1 jit_solution(9882392251464032291)
XLA Ops:
  0.6 1.5 %collective-permute-start = (bf16[4,168,256]{2,1,0:T(8,128)(2,1)}, bf16[4,168,256]{2,1,0:T(8,128)(2,1)S(1)}, u32[]{:S(2)}, u32[]{:S(2)}) collective-permute-start(bf16[4,168,256]{2,1,0:T(8,128)(2,1)} %param.4), channel_id=1, source_target_pairs={{0,1},{1,0},{2,3},{3,2},{4,5},{5,4},{6,7},{7,6},{8,9},{9,8},{10,11... | collective-permute-start | bytes 1032200 | tf_op jit(solution)/shard_map/ppermute | solution.py:22
  2.2 1.4 %collective-permute-done = bf16[4,168,256]{2,1,0:T(8,128)(2,1)S(1)} collective-permute-done((bf16[4,168,256]{2,1,0:T(8,128)(2,1)}, bf16[4,168,256]{2,1,0:T(8,128)(2,1)S(1)}, u32[]{:S(2)}, u32[]{:S(2)}) %collective-permute-start) | collective-permute-done | bytes 344096 | tf_op jit(solution)/shard_map/ppermute | solution.py:22
  3.6 0.5 collective-permute-done.1
  4.1 1.2 %broadcast_select_fusion.3 = (bf16[4,168,256]{2,1,0:T(8,128)(2,1)S(1)}, bf16[4,168,256]{2,1,0:T(8,128)(2,1)S(1)}, bf16[4,168,256]{2,1,0:T(8,128)(2,1)S(1)}, bf16[4,168,256]{2,1,0:T(8,128)(2,1)S(1)}) fusion(bf16[4,168,256]{2,1,0:T(8,128)(2,1)} %refs_3_.1, bf16[4,168,256]{2,1,0:T(8,128)(2,1)S(1)} %collective-permute-done.1, pred[]{:T(512)S(6)} %eq.14, ...), kind=kLoop, calls=%fused_computation.11 | loop fusion | flops 688128 | bytes 2752513 | tf_op jit(solution)/shard_map/jit(_where)/select_n | solution.py:288
  5.6 0.2 maximum_maximum_fusion.1
  5.9 2.9 %collective-permute-start.2 = (bf16[6,336,256]{2,1,0:T(8,128)(2,1)S(1)}, bf16[6,336,256]{2,1,0:T(8,128)(2,1)S(1)}, u32[]{:S(2)}, u32[]{:S(2)}) collective-permute-start(bf16[6,336,256]{2,1,0:T(8,128)(2,1)S(1)} %maximum_maximum_fusion.refs_0_), channel_id=1, source_target_pairs={{0,4},{1,13},{2,6},{3,15},{4,8},{5,1},{6,10},{7,3},{8,12},{9,5},{1... | collective-permute-start | bytes 3096584 | tf_op jit(solution)/shard_map/ppermute | solution.py:22
  8.8 3.6 %collective-permute-start.3 = (bf16[3,336,256]{2,1,0:T(8,128)(2,1)S(1)}, bf16[3,336,256]{2,1,0:T(8,128)(2,1)S(1)}, u32[]{:S(2)}, u32[]{:S(2)}) collective-permute-start(bf16[3,336,256]{2,1,0:T(8,128)(2,1)S(1)} %get-tuple-element.19), channel_id=1, source_target_pairs={{0,2},{1,3},{2,0},{3,1},{4,6},{5,7},{6,4},{7,5},{8,10},{9,11},{10,... | collective-permute-start | bytes 1548296 | tf_op jit(solution)/shard_map/ppermute | solution.py:22
  12.4 4.5 %collective-permute-start.4 = (bf16[336,384]{1,0:T(8,128)(2,1)S(1)}, bf16[336,384]{1,0:T(8,128)(2,1)S(1)}, u32[]{:S(2)}, u32[]{:S(2)}) collective-permute-start(bf16[336,384]{1,0:T(8,128)(2,1)S(1)} %pad_maximum_fusion.3), channel_id=1, source_target_pairs={{0,0},{1,80},{2,8},{3,88},{4,32},{5,112},{6,40},{7,120},{8,64},{9,... | collective-permute-start | bytes 774152 | tf_op jit(solution)/shard_map/ppermute | solution.py:22
  16.9 4.0 %collective-permute-start.5 = (bf16[336,384]{1,0:T(8,128)(2,1)S(1)}, bf16[336,384]{1,0:T(8,128)(2,1)S(1)}, u32[]{:S(2)}, u32[]{:S(2)}) collective-permute-start(bf16[336,384]{1,0:T(8,128)(2,1)S(1)} %pad_maximum_fusion.4), channel_id=1, source_target_pairs={{0,40},{1,120},{2,32},{3,112},{4,72},{5,24},{6,64},{7,16},{8,104},... | collective-permute-start | bytes 774152 | tf_op jit(solution)/shard_map/ppermute | solution.py:22
  20.9 12.2 %collective-permute-done.4 = bf16[336,384]{1,0:T(8,128)(2,1)S(1)} collective-permute-done((bf16[336,384]{1,0:T(8,128)(2,1)S(1)}, bf16[336,384]{1,0:T(8,128)(2,1)S(1)}, u32[]{:S(2)}, u32[]{:S(2)}) %collective-permute-start.4) | collective-permute-done | bytes 258080 | tf_op jit(solution)/shard_map/ppermute | solution.py:22
  33.5 1.5 %collective-permute-start.10 = (bf16[2,336,384]{2,1,0:T(8,128)(2,1)S(1)}, bf16[2,336,384]{2,1,0:T(8,128)(2,1)S(1)}, u32[]{:S(2)}, u32[]{:S(2)}) collective-permute-start(bf16[2,336,384]{2,1,0:T(8,128)(2,1)S(1)} %pad_maximum_fusion.2.refs_8_), channel_id=1, source_target_pairs={{0,96},{1,97},{2,98},{3,99},{4,100},{5,101},{6,102},{7,103},{8,104... | collective-permute-start | bytes 1548296 | tf_op jit(solution)/shard_map/ppermute | solution.py:22
  35.0 1.4 %collective-permute-start.8 = (bf16[3,336,256]{2,1,0:T(8,128)(2,1)S(1)}, bf16[3,336,256]{2,1,0:T(8,128)(2,1)S(1)}, u32[]{:S(2)}, u32[]{:S(2)}) collective-permute-start(bf16[3,336,256]{2,1,0:T(8,128)(2,1)S(1)} %get-tuple-element.34), channel_id=1, source_target_pairs={{0,2},{1,3},{2,0},{3,1},{4,6},{5,7},{6,4},{7,5},{8,10},{9,11},{10,... | collective-permute-start | bytes 1548296 | tf_op jit(solution)/shard_map/ppermute | solution.py:22
  36.4 0.1 pad_maximum_fusion
  36.6 2.1 %collective-permute-start.6 = (bf16[9,336,256]{2,1,0:T(8,128)(2,1)S(1)}, bf16[9,336,256]{2,1,0:T(8,128)(2,1)S(1)}, u32[]{:S(2)}, u32[]{:S(2)}) collective-permute-start(bf16[9,336,256]{2,1,0:T(8,128)(2,1)S(1)} %pad_maximum_fusion), channel_id=1, source_target_pairs={{0,1},{1,0},{2,3},{3,2},{4,5},{5,4},{6,7},{7,6},{8,9},{9,8},{10,11... | collective-permute-start | bytes 4644872 | tf_op jit(solution)/shard_map/ppermute | solution.py:22
  38.6 8.6 %collective-permute-done.10.refs_10_ = bf16[2,336,384]{2,1,0:T(8,128)(2,1)S(1)} collective-permute-done((bf16[2,336,384]{2,1,0:T(8,128)(2,1)S(1)}, bf16[2,336,384]{2,1,0:T(8,128)(2,1)S(1)}, u32[]{:S(2)}, u32[]{:S(2)}) %collective-permute-start.10) | collective-permute-done | bytes 516128 | tf_op jit(solution)/shard_map/ppermute | solution.py:22
  47.2 1.9 %collective-permute-done.9.refs_9_ = bf16[2,336,384]{2,1,0:T(8,128)(2,1)S(1)} collective-permute-done((bf16[2,336,384]{2,1,0:T(8,128)(2,1)S(1)}, bf16[2,336,384]{2,1,0:T(8,128)(2,1)S(1)}, u32[]{:S(2)}, u32[]{:S(2)}) %collective-permute-start.9) | collective-permute-done | bytes 516128 | tf_op jit(solution)/shard_map/ppermute | solution.py:22
  49.2 0.3 collective-permute-done.8.refs_5_.refs_10_
  49.5 1.2 %collective-permute-start.11 = (bf16[2,3,336,256]{3,2,1,0:T(8,128)(2,1)S(1)}, bf16[2,3,336,256]{3,2,1,0:T(8,128)(2,1)S(1)}, u32[]{:S(2)}, u32[]{:S(2)}) collective-permute-start(bf16[2,3,336,256]{3,2,1,0:T(8,128)(2,1)S(1)} %collective-permute-done.7.refs_3_.refs_8_), channel_id=1, source_target_pairs={{0,1},{1,0},{2,3},{3,2},{4,5},{5,4},{6,7},{7,6},{8,9},{9,8},{10,11... | collective-permute-start | bytes 3096584 | tf_op jit(solution)/shard_map/ppermute | solution.py:22
  50.7 1.5 %collective-permute-start.14 = (bf16[3,336,256]{2,1,0:T(8,128)(2,1)S(1)}, bf16[3,336,256]{2,1,0:T(8,128)(2,1)S(1)}, u32[]{:S(2)}, u32[]{:S(2)}) collective-permute-start(bf16[3,336,256]{2,1,0:T(8,128)(2,1)S(1)} %bitcast_select_fusion), channel_id=1, source_target_pairs={{0,8},{1,3},{2,10},{3,1},{4,12},{5,7},{6,14},{7,5},{8,0},{9,11},{1... | collective-permute-start | bytes 1548296 | tf_op jit(solution)/shard_map/ppermute | solution.py:22
  52.3 2.7 %collective-permute-start.13 = (bf16[2,336,384]{2,1,0:T(8,128)(2,1)S(1)}, bf16[2,336,384]{2,1,0:T(8,128)(2,1)S(1)}, u32[]{:S(2)}, u32[]{:S(2)}) collective-permute-start(bf16[2,336,384]{2,1,0:T(8,128)(2,1)S(1)} %broadcast_select_fusion), channel_id=1, source_target_pairs={{0,32},{1,97},{2,34},{3,99},{4,36},{5,101},{6,38},{7,103},{8,40},{... | collective-permute-start | bytes 1548296 | tf_op jit(solution)/shard_map/ppermute | solution.py:22
  55.1 7.2 %shard_map.50 = (f32[3,256,256]{2,1,0:T(8,128)S(1)}, f32[384,768]{1,0:T(8,128)S(1)}, bf16[3,2688,256]{2,1,0:T(8,128)(2,1)S(1)}, bf16[2688,384]{1,0:T(8,128)(2,1)S(1)}) custom-call(bf16[6,336,256]{2,1,0:T(8,128)(2,1)S(1)} %maximum_maximum_fusion.refs_0_, bf16[6,336,256]{2,1,0:T(8,128)(2,1)S(1)} %collective-permute-done.2.refs_1_, ...), custom_call_target="tpu_custom_call" | custom-call | flops 4000000000 | bytes 15000000 | tf_op jit(solution)/shard_map/pallas_call | solution.py:316
  62.4 1.5 %shard_map.51.refs_5_ = f32[384,768]{1,0:T(8,128)S(1)} custom-call(f32[384,768]{1,0:T(8,128)S(1)} %get-tuple-element.30.pair_ref, bf16[3,2688,256]{2,1,0:T(8,128)(2,1)S(1)} %get-tuple-element.31.v_in, bf16[2,336,384]{2,1,0:T(8,128)(2,1)S(1)} %collective-permute-done.13.last_col.refs_7_), custom_call_target="tpu_custom_call" | custom-call | flops 800000000 | bytes 4000000 | tf_op jit(solution)/shard_map/pallas_call | solution.py:333
  64.0 0.3 collective-permute-done.15.refs_14_
  64.3 9.6 %shard_map.52 = (bf16[4,2,2688,256]{3,2,1,0:T(8,128)(2,1)}, bf16[4,168,2688]{2,1,0:T(8,128)(2,1)}) custom-call(s32[32]{0:T(128)S(1)} %copy-done.1, bf16[6,336,256]{2,1,0:T(8,128)(2,1)S(1)} %maximum_maximum_fusion.refs_0_, bf16[6,336,256]{2,1,0:T(8,128)(2,1)S(1)} %collective-permute-done.2.refs_1_, bf16[9,336,256]{2,1,0:T(8,128)(2,1)S(1)} %collective-permute-done.6.refs_2_, ...), custom_call_target="tpu_custom_call" | custom-call | flops 6000000000 | bytes 25000000 | tf_op jit(solution)/shard_map/pallas_call | solution.py:346
  (40 shorter events, 1.0 us)
Async XLA Ops:
  0.6 3.0 %collective-permute-start = (bf16[4,168,256]{2,1,0:T(8,128)(2,1)}, bf16[4,168,256]{2,1,0:T(8,128)(2,1)S(1)}, u32[]{:S(2)}, u32[]{:S(2)}) collective-permute-start(bf16[4,168,256]{2,1,0:T(8,128)(2,1)} %param.4), channel_id=1, source_target_pairs={{0,1},{1,0},{2,3},{3,2},{4,5},{5,4},{6,7},{7,6},{8,9},{9,8},{10,11... | collective-permute-start | bytes 1032200 | tf_op jit(solution)/shard_map/ppermute | solution.py:22
  2.1 2.0 %collective-permute-start.1 = (bf16[4,168,256]{2,1,0:T(8,128)(2,1)}, bf16[4,168,256]{2,1,0:T(8,128)(2,1)S(1)}, u32[]{:S(2)}, u32[]{:S(2)}) collective-permute-start(bf16[4,168,256]{2,1,0:T(8,128)(2,1)} %refs_3_.1), channel_id=1, source_target_pairs={{0,1},{1,0},{2,3},{3,2},{4,5},{5,4},{6,7},{7,6},{8,9},{9,8},{10,11... | collective-permute-start | bytes 1032200 | tf_op jit(solution)/shard_map/ppermute | solution.py:22
  5.9 27.2 %collective-permute-start.2 = (bf16[6,336,256]{2,1,0:T(8,128)(2,1)S(1)}, bf16[6,336,256]{2,1,0:T(8,128)(2,1)S(1)}, u32[]{:S(2)}, u32[]{:S(2)}) collective-permute-start(bf16[6,336,256]{2,1,0:T(8,128)(2,1)S(1)} %maximum_maximum_fusion.refs_0_), channel_id=1, source_target_pairs={{0,4},{1,13},{2,6},{3,15},{4,8},{5,1},{6,10},{7,3},{8,12},{9,5},{1... | collective-permute-start | bytes 3096584 | tf_op jit(solution)/shard_map/ppermute | solution.py:22
  8.8 24.3 %collective-permute-start.3 = (bf16[3,336,256]{2,1,0:T(8,128)(2,1)S(1)}, bf16[3,336,256]{2,1,0:T(8,128)(2,1)S(1)}, u32[]{:S(2)}, u32[]{:S(2)}) collective-permute-start(bf16[3,336,256]{2,1,0:T(8,128)(2,1)S(1)} %get-tuple-element.19), channel_id=1, source_target_pairs={{0,2},{1,3},{2,0},{3,1},{4,6},{5,7},{6,4},{7,5},{8,10},{9,11},{10,... | collective-permute-start | bytes 1548296 | tf_op jit(solution)/shard_map/ppermute | solution.py:22
  12.4 20.7 %collective-permute-start.4 = (bf16[336,384]{1,0:T(8,128)(2,1)S(1)}, bf16[336,384]{1,0:T(8,128)(2,1)S(1)}, u32[]{:S(2)}, u32[]{:S(2)}) collective-permute-start(bf16[336,384]{1,0:T(8,128)(2,1)S(1)} %pad_maximum_fusion.3), channel_id=1, source_target_pairs={{0,0},{1,80},{2,8},{3,88},{4,32},{5,112},{6,40},{7,120},{8,64},{9,... | collective-permute-start | bytes 774152 | tf_op jit(solution)/shard_map/ppermute | solution.py:22
  16.9 16.2 %collective-permute-start.5 = (bf16[336,384]{1,0:T(8,128)(2,1)S(1)}, bf16[336,384]{1,0:T(8,128)(2,1)S(1)}, u32[]{:S(2)}, u32[]{:S(2)}) collective-permute-start(bf16[336,384]{1,0:T(8,128)(2,1)S(1)} %pad_maximum_fusion.4), channel_id=1, source_target_pairs={{0,40},{1,120},{2,32},{3,112},{4,72},{5,24},{6,64},{7,16},{8,104},... | collective-permute-start | bytes 774152 | tf_op jit(solution)/shard_map/ppermute | solution.py:22
  33.4 16.1 %collective-permute-start.7 = (bf16[2,3,336,256]{3,2,1,0:T(8,128)(2,1)S(1)}, bf16[2,3,336,256]{3,2,1,0:T(8,128)(2,1)S(1)}, u32[]{:S(2)}, u32[]{:S(2)}) collective-permute-start(bf16[2,3,336,256]{3,2,1,0:T(8,128)(2,1)S(1)} %pad_maximum_fusion.1), channel_id=1, source_target_pairs={{0,4},{1,13},{2,6},{3,15},{4,8},{5,1},{6,10},{7,3},{8,12},{9,5},{1... | collective-permute-start | bytes 3096584 | tf_op jit(solution)/shard_map/ppermute | solution.py:22
  33.5 13.8 %collective-permute-start.10 = (bf16[2,336,384]{2,1,0:T(8,128)(2,1)S(1)}, bf16[2,336,384]{2,1,0:T(8,128)(2,1)S(1)}, u32[]{:S(2)}, u32[]{:S(2)}) collective-permute-start(bf16[2,336,384]{2,1,0:T(8,128)(2,1)S(1)} %pad_maximum_fusion.2.refs_8_), channel_id=1, source_target_pairs={{0,96},{1,97},{2,98},{3,99},{4,100},{5,101},{6,102},{7,103},{8,104... | collective-permute-start | bytes 1548296 | tf_op jit(solution)/shard_map/ppermute | solution.py:22
  35.0 14.2 %collective-permute-start.9 = (bf16[2,336,384]{2,1,0:T(8,128)(2,1)S(1)}, bf16[2,336,384]{2,1,0:T(8,128)(2,1)S(1)}, u32[]{:S(2)}, u32[]{:S(2)}) collective-permute-start(bf16[2,336,384]{2,1,0:T(8,128)(2,1)S(1)} %pad_maximum_fusion.2.refs_8_), channel_id=1, source_target_pairs={{0,32},{1,33},{2,34},{3,35},{4,36},{5,37},{6,38},{7,39},{8,40},{9,... | collective-permute-start | bytes 1548296 | tf_op jit(solution)/shard_map/ppermute | solution.py:22
  35.0 14.5 %collective-permute-start.8 = (bf16[3,336,256]{2,1,0:T(8,128)(2,1)S(1)}, bf16[3,336,256]{2,1,0:T(8,128)(2,1)S(1)}, u32[]{:S(2)}, u32[]{:S(2)}) collective-permute-start(bf16[3,336,256]{2,1,0:T(8,128)(2,1)S(1)} %get-tuple-element.34), channel_id=1, source_target_pairs={{0,2},{1,3},{2,0},{3,1},{4,6},{5,7},{6,4},{7,5},{8,10},{9,11},{10,... | collective-permute-start | bytes 1548296 | tf_op jit(solution)/shard_map/ppermute | solution.py:22
  36.6 18.5 %collective-permute-start.6 = (bf16[9,336,256]{2,1,0:T(8,128)(2,1)S(1)}, bf16[9,336,256]{2,1,0:T(8,128)(2,1)S(1)}, u32[]{:S(2)}, u32[]{:S(2)}) collective-permute-start(bf16[9,336,256]{2,1,0:T(8,128)(2,1)S(1)} %pad_maximum_fusion), channel_id=1, source_target_pairs={{0,1},{1,0},{2,3},{3,2},{4,5},{5,4},{6,7},{7,6},{8,9},{9,8},{10,11... | collective-permute-start | bytes 4644872 | tf_op jit(solution)/shard_map/ppermute | solution.py:22
  49.5 5.6 %collective-permute-start.11 = (bf16[2,3,336,256]{3,2,1,0:T(8,128)(2,1)S(1)}, bf16[2,3,336,256]{3,2,1,0:T(8,128)(2,1)S(1)}, u32[]{:S(2)}, u32[]{:S(2)}) collective-permute-start(bf16[2,3,336,256]{3,2,1,0:T(8,128)(2,1)S(1)} %collective-permute-done.7.refs_3_.refs_8_), channel_id=1, source_target_pairs={{0,1},{1,0},{2,3},{3,2},{4,5},{5,4},{6,7},{7,6},{8,9},{9,8},{10,11... | collective-permute-start | bytes 3096584 | tf_op jit(solution)/shard_map/ppermute | solution.py:22
  50.7 4.4 %collective-permute-start.12 = (bf16[3,336,256]{2,1,0:T(8,128)(2,1)S(1)}, bf16[3,336,256]{2,1,0:T(8,128)(2,1)S(1)}, u32[]{:S(2)}, u32[]{:S(2)}) collective-permute-start(bf16[3,336,256]{2,1,0:T(8,128)(2,1)S(1)} %collective-permute-done.8.refs_5_.refs_10_), channel_id=1, source_target_pairs={{0,1},{1,0},{2,3},{3,2},{4,5},{5,4},{6,7},{7,6},{8,9},{9,8},{10,11... | collective-permute-start | bytes 1548296 | tf_op jit(solution)/shard_map/ppermute | solution.py:22
  50.7 11.6 %collective-permute-start.14 = (bf16[3,336,256]{2,1,0:T(8,128)(2,1)S(1)}, bf16[3,336,256]{2,1,0:T(8,128)(2,1)S(1)}, u32[]{:S(2)}, u32[]{:S(2)}) collective-permute-start(bf16[3,336,256]{2,1,0:T(8,128)(2,1)S(1)} %bitcast_select_fusion), channel_id=1, source_target_pairs={{0,8},{1,3},{2,10},{3,1},{4,12},{5,7},{6,14},{7,5},{8,0},{9,11},{1... | collective-permute-start | bytes 1548296 | tf_op jit(solution)/shard_map/ppermute | solution.py:22
  52.3 10.1 %collective-permute-start.13 = (bf16[2,336,384]{2,1,0:T(8,128)(2,1)S(1)}, bf16[2,336,384]{2,1,0:T(8,128)(2,1)S(1)}, u32[]{:S(2)}, u32[]{:S(2)}) collective-permute-start(bf16[2,336,384]{2,1,0:T(8,128)(2,1)S(1)} %broadcast_select_fusion), channel_id=1, source_target_pairs={{0,32},{1,97},{2,34},{3,99},{4,36},{5,101},{6,38},{7,103},{8,40},{... | collective-permute-start | bytes 1548296 | tf_op jit(solution)/shard_map/ppermute | solution.py:22
  62.3 2.0 %collective-permute-start.15 = (bf16[3,336,256]{2,1,0:T(8,128)(2,1)S(1)}, bf16[3,336,256]{2,1,0:T(8,128)(2,1)S(1)}, u32[]{:S(2)}, u32[]{:S(2)}) collective-permute-start(bf16[3,336,256]{2,1,0:T(8,128)(2,1)S(1)} %collective-permute-done.14.refs_11_), channel_id=1, source_target_pairs={{0,1},{1,0},{2,3},{3,2},{4,5},{5,4},{6,7},{7,6},{8,9},{9,8},{10,11... | collective-permute-start | bytes 1548296 | tf_op jit(solution)/shard_map/ppermute | solution.py:22
  62.4 1.9 %copy-start = (bf16[4,168,256]{2,1,0:T(8,128)(2,1)S(1)}, bf16[4,168,256]{2,1,0:T(8,128)(2,1)}, u32[]{:S(2)}) copy-start(bf16[4,168,256]{2,1,0:T(8,128)(2,1)} %refs_3_.1) | copy-start | bytes 1032196
  62.4 1.9 %copy-start.1 = (s32[32]{0:T(128)S(1)}, s32[32]{0:T(128)}, u32[]{:S(2)}) copy-start(s32[32]{0:T(128)} %rank_ref.1) | copy-start | bytes 388
